TPU v7x, 256 devices: a whole 4x4x8 slice. The times are simulated.
256 devices in a mesh: section: 16 (over x_lo, y, core), dp: 16 (over x_hi, z).
Axes of the slice: x: 4 (x_hi: 2, x_lo: 2; x = x_hi * 2 + x_lo), y: 4, z: 8, core: 2. Of those that a mesh axis runs over, the one named last changes fastest.
Arguments:
- activations: bfloat16 [16, 16, 256, 4096], P('section', 'dp'), may hold values from -6 to 6
- gains: float32 [2, 16, 4096], P(None, 'section'), may hold values from 0.1 to 1.9
- kv_weight: bfloat16 [2, 16, 4096, 1024], P(None, 'section', 'dp'), as said below
- lengths: int32 [16, 16], P('section', 'dp'), may hold values from 64 to 256
Outputs:
- advanced: bfloat16 [16, 16, 256, 4096], P('section', 'dp')
Inputs may be any that keep to these rules, and one draw needn't show every extreme that they name: `kv_weight`: projection weights of order one to eight over square root of 4096.
All inputs are finite; a program needn't handle non-finite values.
Results may differ from a plain program's by a relative error of at most 0.022.
Values may be sent and summed in bfloat16 or wider, within the bound.
A program may use at most 128 MiB of HBM per device.

v0:
```python
import jax
import jax.numpy as jnp
from jax import lax
from jax.sharding import PartitionSpec as P

HEAD_DIM = 128
TICKS = 3


def from_behind(shard, axis, by):
    peers = lax.axis_size(axis)
    return lax.ppermute(shard, axis, [(i, (i + by) % peers) for i in range(peers)])


def normalize(block, gain):
    xf = block.astype(jnp.float32)
    factor = lax.rsqrt(jnp.mean(xf * xf, axis=-1, keepdims=True) + 1e-05)
    return (xf, (xf * factor * gain).astype(jnp.bfloat16))


def finish(xf, normed, keyval, length):
    seq = normed.shape[0]
    width = keyval.shape[1] // 2
    groups = width // HEAD_DIM
    keys = keyval[:, :width].reshape(seq, groups, HEAD_DIM)
    values = keyval[:, width:].reshape(seq, groups, HEAD_DIM)
    query = normed.reshape(seq, groups, -1, HEAD_DIM)
    scores = jnp.einsum(
        "qhgd,khd->hgqk", query, keys, preferred_element_type=jnp.float32
    ) * HEAD_DIM ** (-0.5)
    places = jnp.arange(seq, dtype=jnp.int32)
    allowed = (places[None, :] <= places[:, None]) & (places[None, :] < length)
    scores = jnp.where(allowed, scores, -1e30)
    topmost = jnp.max(scores, axis=-1, keepdims=True)
    expo = jnp.exp(scores - topmost)
    probs = (expo / jnp.sum(expo, axis=-1, keepdims=True)).astype(jnp.bfloat16)
    mixed = jnp.einsum("hgqk,khd->qhgd", probs, values, preferred_element_type=jnp.float32).reshape(
        seq, -1
    )
    return (xf + mixed).astype(jnp.bfloat16)


def per_device(activations, gains, kv_weight, lengths):
    block = activations[0, 0]
    length = lengths[0, 0]
    section = lax.axis_index("section")
    local_rows = kv_weight[:, 0]
    gain_rows = gains[:, 0]
    for tick in range(TICKS):
        repeat = (section < tick).astype(jnp.int32)
        gain = lax.dynamic_index_in_dim(gain_rows, repeat, 0, keepdims=False)
        xf, normed = normalize(block, gain)
        shard_rows = lax.dynamic_index_in_dim(local_rows, repeat, 0, keepdims=False)

        def add_rows(total, piece, start, normed=normed):
            return jnp.dot(normed, piece, preferred_element_type=jnp.float32)

        empty = jnp.zeros((normed.shape[0], shard_rows.shape[1]), jnp.float32)
        keyval = add_rows(empty, lax.all_gather(shard_rows, "dp", axis=0, tiled=True), jnp.int32(0))
        block = finish(xf, normed, keyval.astype(jnp.bfloat16), length)
        block, length = from_behind((block, length), "section", 1)
    return block[None, None]


def solution(mesh):
    return jax.shard_map(
        per_device,
        mesh=mesh,
        in_specs=(
            P("section", "dp", None, None),
            P(None, "section", None),
            P(None, "section", "dp", None),
            P("section", "dp"),
        ),
        out_specs=P("section", "dp", None, None),
        check_vma=False,
    )
```

profile of v0, /device:TPU:2, one launch (start us, length us, event | category | flops | bytes accessed | tf_op | source)
XLA Modules:
  0.0 476.3 jit_solution(14156711579204725986)
XLA Ops:
  6.5 2.8 constant_dynamic-slice_fusion.4
  12.5 2.7 copy.38
  15.4 132.4 %all-gather.7.cloned.1.call-done = bf16[1,1,4096,1024]{3,2,1,0:T(8,128)(2,1)} async-done(((bf16[1,1,256,1024]{3,2,1,0:T(8,128)(2,1)}), bf16[1,1,4096,1024]{3,2,1,0:T(8,128)(2,1)}) %all-gather.7.cloned.1.call-update) | async-done | bytes 8388624 | tf_op jit(solution)/shard_map/all_gather | solution.py:59
  147.8 5.7 %fusion.52 = bf16[256,1024]{1,0:T(8,128)(2,1)S(1)} fusion(bf16[1,1,4096,1024]{3,2,1,0:T(8,128)(2,1)} %all-gather.7.cloned.1.call-done, bf16[1,1,256,4096]{3,2,1,0:T(8,128)(2,1)S(1)} %copy-done, f32[4096]{0:T(1024)S(1)} %bitcast.131, f32[256]{0:T(256)S(1)} %add_rsqrt_fusion.2), kind=kOutput, calls=%fused_computation.68 | convolution fusion | flops 2151940096 | bytes 11027456 | tf_op jit(solution)/shard_map/dot_general | solution.py:56
  153.8 5.2 %fusion.41 = f32[4,256,256,8]{2,1,3,0:T(8,128)S(1)} fusion(f32[256,4,8,128]{3,2,1,0:T(8,128)} %bitcast.118, f32[4,8,128]{2,1,0:T(8,128)S(1)} %bitcast.132, f32[256]{0:T(256)S(1)} %add_rsqrt_fusion.2, bf16[256,4,128,1]{2,1,0,3:T(4,128)(2,1)S(1)} %bitcast.125), kind=kOutput, calls=%fused_computation.59 | convolution fusion | flops 540016640 | bytes 12862464 | tf_op jit(solution)/shard_map/qhgd,khd->hgqk/dot_general | solution.py:28
  161.4 2.7 fusion.35
  164.2 5.6 %copy.9 = f32[256,4096]{1,0:T(8,128)} copy(f32[256,4096]{0,1:T(8,128)} %bitcast.121) | data formatting | bytes 8388608 | tf_op jit(solution)/shard_map/reshape | solution.py:37
  169.8 2.8 fusion.18
  174.2 26.1 %collective-permute-done.1 = s32[]{:T(128)} collective-permute-done((s32[]{:T(128)}, s32[]{:T(128)}, u32[]{:S(2)}, u32[]{:S(2)}) %collective-permute-start.1) | collective-permute-done | bytes 36 | tf_op jit(solution)/shard_map/ppermute | solution.py:12
  204.1 78.9 %all-gather.9.cloned.1.call-done = bf16[1,1,4096,1024]{3,2,1,0:T(8,128)(2,1)} async-done(((bf16[1,1,256,1024]{3,2,1,0:T(8,128)(2,1)}), bf16[1,1,4096,1024]{3,2,1,0:T(8,128)(2,1)}) %all-gather.9.cloned.1.call-update) | async-done | bytes 8388624 | tf_op jit(solution)/shard_map/all_gather | solution.py:59
  283.1 5.7 %fusion.57 = bf16[256,1024]{1,0:T(8,128)(2,1)S(1)} fusion(bf16[1,1,4096,1024]{3,2,1,0:T(8,128)(2,1)} %all-gather.9.cloned.1.call-done, bf16[256,4096]{1,0:T(8,128)(2,1)S(1)} %collective-permute-done, f32[4096]{0:T(1024)S(1)} %bitcast.136, f32[256]{0:T(256)S(1)} %add_rsqrt_fusion.1), kind=kOutput, calls=%fused_computation.69 | convolution fusion | flops 2151940096 | bytes 11027456 | tf_op jit(solution)/shard_map/dot_general | solution.py:56
  289.1 2.9 fusion.46
  292.0 2.4 fusion.83
  294.4 2.8 fusion.36
  297.2 5.7 %copy.14 = f32[256,4096]{1,0:T(8,128)} copy(f32[256,4096]{0,1:T(8,128)} %bitcast.122) | data formatting | bytes 8388608 | tf_op jit(solution)/shard_map/reshape | solution.py:37
  302.8 2.8 fusion.22
  307.3 26.1 %collective-permute-done.3 = s32[]{:T(128)} collective-permute-done((s32[]{:T(128)}, s32[]{:T(128)}, u32[]{:S(2)}, u32[]{:S(2)}) %collective-permute-start.3) | collective-permute-done | bytes 36 | tf_op jit(solution)/shard_map/ppermute | solution.py:12
  337.2 81.1 %all-gather.11.cloned.1.call-done = bf16[1,1,4096,1024]{3,2,1,0:T(8,128)(2,1)} async-done(((bf16[1,1,256,1024]{3,2,1,0:T(8,128)(2,1)}), bf16[1,1,4096,1024]{3,2,1,0:T(8,128)(2,1)}) %all-gather.11.cloned.1.call-update) | async-done | bytes 8388624 | tf_op jit(solution)/shard_map/all_gather | solution.py:59
  418.3 5.7 %fusion.60 = bf16[256,1024]{1,0:T(8,128)(2,1)S(1)} fusion(bf16[1,1,4096,1024]{3,2,1,0:T(8,128)(2,1)} %all-gather.11.cloned.1.call-done, bf16[256,4096]{1,0:T(8,128)(2,1)S(1)} %collective-permute-done.2, f32[4096]{0:T(1024)S(1)} %bitcast.134, f32[256]{0:T(256)S(1)} %add_rsqrt_fusion), kind=kOutput, calls=%fused_computation.70 | convolution fusion | flops 2151940096 | bytes 11027456 | tf_op jit(solution)/shard_map/dot_general | solution.py:56
  424.4 2.9 fusion.44
  429.7 2.7 fusion.37
  432.4 5.6 %copy.19 = f32[256,4096]{1,0:T(8,128)} copy(f32[256,4096]{0,1:T(8,128)} %bitcast.123) | data formatting | bytes 8388608 | tf_op jit(solution)/shard_map/reshape | solution.py:37
  438.0 2.7 fusion.26
  440.9 27.6 %collective-permute-done.4 = bf16[256,4096]{1,0:T(8,128)(2,1)S(1)} collective-permute-done((bf16[256,4096]{1,0:T(8,128)(2,1)S(1)}, bf16[256,4096]{1,0:T(8,128)(2,1)S(1)}, u32[]{:S(2)}, u32[]{:S(2)}) %collective-permute-start.4) | collective-permute-done | bytes 2097184 | tf_op jit(solution)/shard_map/ppermute | solution.py:12
  (47 shorter events, 20.3 us)
Async XLA Ops:
  6.5 4.3 copy-start
  6.5 141.3 %all-gather.7.cloned.1.call-start = ((), (), s32[]{:S(2)}) async-start(), calls=%async_computation | async-start | bytes 8912896 | tf_op jit(solution)/shard_map/all_gather | solution.py:59
  9.4 273.7 %all-gather.9.cloned.1.call-start = ((), (), s32[]{:S(2)}) async-start(), calls=%async_computation.1 | async-start | bytes 8912896 | tf_op jit(solution)/shard_map/all_gather | solution.py:59
  10.1 408.2 %all-gather.11.cloned.1.call-start = ((), (), s32[]{:S(2)}) async-start(), calls=%async_computation.2 | async-start | bytes 8912896 | tf_op jit(solution)/shard_map/all_gather | solution.py:59
  12.5 2.8 copy-start.1
  172.6 28.5 %collective-permute-start = (bf16[256,4096]{1,0:T(8,128)(2,1)S(1)}, bf16[256,4096]{1,0:T(8,128)(2,1)S(1)}, u32[]{:S(2)}, u32[]{:S(2)}) collective-permute-start(bf16[256,4096]{1,0:T(8,128)(2,1)S(1)} %fusion.18), channel_id=1, source_target_pairs={{0,16},{16,32},{32,48},{48,64},{64,80},{80,96},{96,112},{112,128},... | collective-permute-start | bytes 6291464 | tf_op jit(solution)/shard_map/ppermute | solution.py:12
  172.7 27.7 %collective-permute-start.1 = (s32[]{:T(128)}, s32[]{:T(128)}, u32[]{:S(2)}, u32[]{:S(2)}) collective-permute-start(s32[]{:T(128)} %bitcast.6), channel_id=1, source_target_pairs={{0,16},{16,32},{32,48},{48,64},{64,80},{80,96},{96,112},{112,128},... | collective-permute-start | bytes 20 | tf_op jit(solution)/shard_map/ppermute | solution.py:12
  305.6 28.5 %collective-permute-start.2 = (bf16[256,4096]{1,0:T(8,128)(2,1)S(1)}, bf16[256,4096]{1,0:T(8,128)(2,1)S(1)}, u32[]{:S(2)}, u32[]{:S(2)}) collective-permute-start(bf16[256,4096]{1,0:T(8,128)(2,1)S(1)} %fusion.22), channel_id=1, source_target_pairs={{0,16},{16,32},{32,48},{48,64},{64,80},{80,96},{96,112},{112,128},... | collective-permute-start | bytes 6291464 | tf_op jit(solution)/shard_map/ppermute | solution.py:12
  305.7 27.7 %collective-permute-start.3 = (s32[]{:T(128)}, s32[]{:T(128)}, u32[]{:S(2)}, u32[]{:S(2)}) collective-permute-start(s32[]{:T(128)} %collective-permute-done.1), channel_id=1, source_target_pairs={{0,16},{16,32},{32,48},{48,64},{64,80},{80,96},{96,112},{112,128},... | collective-permute-start | bytes 20 | tf_op jit(solution)/shard_map/ppermute | solution.py:12
  440.8 27.6 %collective-permute-start.4 = (bf16[256,4096]{1,0:T(8,128)(2,1)S(1)}, bf16[256,4096]{1,0:T(8,128)(2,1)S(1)}, u32[]{:S(2)}, u32[]{:S(2)}) collective-permute-start(bf16[256,4096]{1,0:T(8,128)(2,1)S(1)} %fusion.26), channel_id=1, source_target_pairs={{0,16},{16,32},{32,48},{48,64},{64,80},{80,96},{96,112},{112,128},... | collective-permute-start | bytes 6291464 | tf_op jit(solution)/shard_map/ppermute | solution.py:12
Sparse Core Ops, SparseCore 0:
  9.9 137.8 all-gather.6
  150.4 132.6 all-gather.8
  285.7 132.6 all-gather.10
where the time goes:
time: 477 us; the launch traced here: 476 us
  waiting for transfers between devices  374 us (78%)
  matrix products  36.6 us (8%)
  local copies, waits for them, and re-layouts  28.1 us (6%)
  other arithmetic  20.3 us (4%)
  between operations  14 us (3%)
    all_gather x3, waiting for transfers between devices, per_device(): lax.all_gather(shard_rows, 'dp', axis=0, tiled=True)  293 us
    ppermute x5, waiting for transfers between devices, from_behind(): lax.ppermute(shard, axis, [(i, (i + by) % peers) for i in range(peers)])  79.8 us
    dot_general x3, matrix products, add_rows(): return jnp.dot(normed, piece, preferred_element_type=jnp.float32)  17.2 us
    reshape x3, local copies, waits for them, and re-layouts, finish(): jnp.einsum('hgqk,khd->qhgd', probs, values, preferred_element_type=jnp.fl...  16.9 us
    dot_general x3, matrix products, finish(): jnp.einsum('qhgd,khd->hgqk', query, keys, preferred_element_type=jnp.floa...  11.1 us
  transfers between devices with their start and end apart: 8, of which 6 were waited for; matrix products, arithmetic and copies ran while one was open for 12% of the time, Pallas kernels for 0%

commit v1 on v0

--- a/solution.py
+++ b/solution.py
@@ -56,7 +56,13 @@
             return jnp.dot(normed, piece, preferred_element_type=jnp.float32)
 
         empty = jnp.zeros((normed.shape[0], shard_rows.shape[1]), jnp.float32)
-        keyval = add_rows(empty, lax.all_gather(shard_rows, "dp", axis=0, tiled=True), jnp.int32(0))
+        keyval = add_rows(
+            empty,
+            jnp.concatenate(
+                lax.all_to_all(jnp.stack([shard_rows] * lax.axis_size("dp")), "dp", 0, 0), axis=0
+            ),
+            jnp.int32(0),
+        )
         block = finish(xf, normed, keyval.astype(jnp.bfloat16), length)
         block, length = from_behind((block, length), "section", 1)
     return block[None, None]

time: 477 us -> 662 us (1.39); the launches traced: 476 us -> 652 us
  blocking collectives: 0 us -> 196 us
  waiting for transfers between devices: 374 us -> 331 us
  starting transfers between devices: 3.51 us -> 26.1 us
  between operations: 14 us -> 0.96 us
  local copies, waits for them, and re-layouts: 28.1 us -> 39 us
    all_gather x3 -> x0, waiting for transfers between devices: 293 us -> none  [per_device(): lax.all_gather(shard_rows, 'dp', axis=0, tiled=True)]
    all_to_all x0 -> x2, waiting for transfers between devices: none -> 214 us  [per_device(): lax.all_to_all(jnp.stack([shard_rows] * lax.axis_size('dp')), 'dp', 0, 0)]
    all_to_all x0 -> x1, blocking collectives: none -> 196 us  [per_device(): lax.all_to_all(jnp.stack([shard_rows] * lax.axis_size('dp')), 'dp', 0, 0)]
    ppermute x5, waiting for transfers between devices: 79.8 us -> 117 us  [from_behind(): lax.ppermute(shard, axis, [(i, (i + by) % peers) for i in range(peers)])]
    all_to_all x0 -> x2, starting transfers between devices: none -> 23.8 us  [per_device(): lax.all_to_all(jnp.stack([shard_rows] * lax.axis_size('dp')), 'dp', 0, 0)]
    another operation x0 -> x3, local copies, waits for them, and re-layouts: none -> 9.67 us  [per_device(): jnp.stack([shard_rows] * lax.axis_size('dp'))]
  transfers between devices with their start and end apart: 8 -> 7, of which waited for: 6 -> 5; matrix products, arithmetic and copies ran while one was open for 12% -> 10% of each run, Pallas kernels for 0% -> 0%
where the time goes in v1:
time: 662 us; the launch traced here: 652 us
  waiting for transfers between devices  331 us (50%)
  blocking collectives  196 us (30%)
  local copies, waits for them, and re-layouts  39 us (6%)
  matrix products  36.6 us (6%)
  starting transfers between devices  26.1 us (4%)
  other arithmetic  22.4 us (3%)
    all_to_all x2, waiting for transfers between devices, per_device(): lax.all_to_all(jnp.stack([shard_rows] * lax.axis_size('dp')), 'dp', 0, 0)  214 us
    all_to_all x1, blocking collectives, per_device(): lax.all_to_all(jnp.stack([shard_rows] * lax.axis_size('dp')), 'dp', 0, 0)  196 us
    ppermute x5, waiting for transfers between devices, from_behind(): lax.ppermute(shard, axis, [(i, (i + by) % peers) for i in range(peers)])  117 us
    all_to_all x2, starting transfers between devices, per_device(): lax.all_to_all(jnp.stack([shard_rows] * lax.axis_size('dp')), 'dp', 0, 0)  23.8 us
    dot_general x3, matrix products, add_rows(): return jnp.dot(normed, piece, preferred_element_type=jnp.float32)  17.2 us
    reshape x3, local copies, waits for them, and re-layouts, finish(): jnp.einsum('hgqk,khd->qhgd', probs, values, preferred_element_type=jnp.fl...  16.9 us
  transfers between devices with their start and end apart: 7, of which 5 were waited for; matrix products, arithmetic and copies ran while one was open for 10% of the time, Pallas kernels for 0%

profile of v1, /device:TPU:2, one launch (start us, length us, event | category | flops | bytes accessed | tf_op | source)
XLA Modules:
  0.0 652.1 jit_solution(11066821373599889095)
XLA Ops:
  3.0 195.8 %all_to_all.15 = bf16[16,256,1024]{2,1,0:T(8,128)(2,1)} all-to-all(bf16[16,256,1024]{2,1,0:T(8,128)(2,1)S(1)} %stack.6), channel_id=1, replica_groups=mesh['section'=16,'dp'=16] {'dp'}, dimensions={0} | all-to-all | bytes 16777216 | tf_op jit(solution)/shard_map/all_to_all | solution.py:62
  198.7 4.3 stack.7
  203.1 4.9 all-to-all-start.1
  211.6 181.0 %all-to-all-done.1 = bf16[16,256,1024]{2,1,0:T(8,128)(2,1)} async-done(((bf16[16,256,1024]{2,1,0:T(8,128)(2,1)}), bf16[16,256,1024]{2,1,0:T(8,128)(2,1)}, u32[]{:S(2)}, u32[]{:S(2)}) %all-to-all-start.1) | async-done | bytes 8388640 | tf_op jit(solution)/shard_map/all_to_all | solution.py:62
  392.6 4.3 stack.8
  396.9 19.0 %all-to-all-start.2 = ((bf16[16,256,1024]{2,1,0:T(8,128)(2,1)}), bf16[16,256,1024]{2,1,0:T(8,128)(2,1)}, u32[]{:S(2)}, u32[]{:S(2)}) async-start(bf16[16,256,1024]{2,1,0:T(8,128)(2,1)} %stack.8), calls=%async_computation.2 | async-start | bytes 16777216 | tf_op jit(solution)/shard_map/all_to_all | solution.py:62
  415.9 4.9 copy.38
  420.9 5.8 fusion.47
  426.9 5.2 fusion.34
  434.5 2.8 fusion.28
  437.3 5.6 copy.9
  442.9 2.7 fusion.9
  447.4 32.2 %collective-permute-done.1 = s32[]{:T(128)} collective-permute-done((s32[]{:T(128)}, s32[]{:T(128)}, u32[]{:S(2)}, u32[]{:S(2)}) %collective-permute-start.1) | collective-permute-done | bytes 36 | tf_op jit(solution)/shard_map/ppermute | solution.py:12
  483.4 5.7 convolution_convert_fusion.1
  489.4 2.9 fusion.41
  497.5 5.6 copy.14
  503.1 2.7 fusion.13
  506.3 57.7 %collective-permute-done.3 = s32[]{:T(128)} collective-permute-done((s32[]{:T(128)}, s32[]{:T(128)}, u32[]{:S(2)}, u32[]{:S(2)}) %collective-permute-start.3) | collective-permute-done | bytes 36 | tf_op jit(solution)/shard_map/ppermute | solution.py:12
  567.7 33.0 %all-to-all-done.2 = bf16[16,256,1024]{2,1,0:T(8,128)(2,1)} async-done(((bf16[16,256,1024]{2,1,0:T(8,128)(2,1)}), bf16[16,256,1024]{2,1,0:T(8,128)(2,1)}, u32[]{:S(2)}, u32[]{:S(2)}) %all-to-all-start.2) | async-done | bytes 8388640 | tf_op jit(solution)/shard_map/all_to_all | solution.py:62
  600.7 5.7 convolution_convert_fusion
  606.7 2.9 fusion.39
  614.7 5.6 copy.19
  620.4 2.7 fusion.17
  623.2 27.6 %collective-permute-done.4 = bf16[256,4096]{1,0:T(8,128)(2,1)S(1)} collective-permute-done((bf16[256,4096]{1,0:T(8,128)(2,1)S(1)}, bf16[256,4096]{1,0:T(8,128)(2,1)S(1)}, u32[]{:S(2)}, u32[]{:S(2)}) %collective-permute-start.4) | collective-permute-done | bytes 2097184 | tf_op jit(solution)/shard_map/ppermute | solution.py:12
  (46 shorter events, 30.5 us)
Async XLA Ops:
  203.0 5.5 copy-start
  203.1 189.6 %all-to-all-start.1 = ((bf16[16,256,1024]{2,1,0:T(8,128)(2,1)}), bf16[16,256,1024]{2,1,0:T(8,128)(2,1)}, u32[]{:S(2)}, u32[]{:S(2)}) async-start(bf16[16,256,1024]{2,1,0:T(8,128)(2,1)} %stack.7), calls=%async_computation.1 | async-start | bytes 16777216 | tf_op jit(solution)/shard_map/all_to_all | solution.py:62
  396.9 203.8 %all-to-all-start.2 = ((bf16[16,256,1024]{2,1,0:T(8,128)(2,1)}), bf16[16,256,1024]{2,1,0:T(8,128)(2,1)}, u32[]{:S(2)}, u32[]{:S(2)}) async-start(bf16[16,256,1024]{2,1,0:T(8,128)(2,1)} %stack.8), calls=%async_computation.2 | async-start | bytes 16777216 | tf_op jit(solution)/shard_map/all_to_all | solution.py:62
  415.9 5.0 copy-start.1
  445.7 34.7 %collective-permute-start = (bf16[256,4096]{1,0:T(8,128)(2,1)S(1)}, bf16[256,4096]{1,0:T(8,128)(2,1)S(1)}, u32[]{:S(2)}, u32[]{:S(2)}) collective-permute-start(bf16[256,4096]{1,0:T(8,128)(2,1)S(1)} %fusion.9), channel_id=1, source_target_pairs={{0,16},{16,32},{32,48},{48,64},{64,80},{80,96},{96,112},{112,128},... | collective-permute-start | bytes 6291464 | tf_op jit(solution)/shard_map/ppermute | solution.py:12
  445.8 33.8 %collective-permute-start.1 = (s32[]{:T(128)}, s32[]{:T(128)}, u32[]{:S(2)}, u32[]{:S(2)}) collective-permute-start(s32[]{:T(128)} %bitcast.8), channel_id=1, source_target_pairs={{0,16},{16,32},{32,48},{48,64},{64,80},{80,96},{96,112},{112,128},... | collective-permute-start | bytes 20 | tf_op jit(solution)/shard_map/ppermute | solution.py:12
  505.8 58.8 %collective-permute-start.2 = (bf16[256,4096]{1,0:T(8,128)(2,1)S(1)}, bf16[256,4096]{1,0:T(8,128)(2,1)S(1)}, u32[]{:S(2)}, u32[]{:S(2)}) collective-permute-start(bf16[256,4096]{1,0:T(8,128)(2,1)S(1)} %fusion.13), channel_id=1, source_target_pairs={{0,16},{16,32},{32,48},{48,64},{64,80},{80,96},{96,112},{112,128},... | collective-permute-start | bytes 6291464 | tf_op jit(solution)/shard_map/ppermute | solution.py:12
  505.9 58.0 %collective-permute-start.3 = (s32[]{:T(128)}, s32[]{:T(128)}, u32[]{:S(2)}, u32[]{:S(2)}) collective-permute-start(s32[]{:T(128)} %collective-permute-done.1), channel_id=1, source_target_pairs={{0,16},{16,32},{32,48},{48,64},{64,80},{80,96},{96,112},{112,128},... | collective-permute-start | bytes 20 | tf_op jit(solution)/shard_map/ppermute | solution.py:12
  623.1 27.6 %collective-permute-start.4 = (bf16[256,4096]{1,0:T(8,128)(2,1)S(1)}, bf16[256,4096]{1,0:T(8,128)(2,1)S(1)}, u32[]{:S(2)}, u32[]{:S(2)}) collective-permute-start(bf16[256,4096]{1,0:T(8,128)(2,1)S(1)} %fusion.17), channel_id=1, source_target_pairs={{0,16},{16,32},{32,48},{48,64},{64,80},{80,96},{96,112},{112,128},... | collective-permute-start | bytes 6291464 | tf_op jit(solution)/shard_map/ppermute | solution.py:12
